TPU v7x, 32 devices: a whole 2x2x4 slice. The times are simulated.
32 devices in a mesh: grp: 2 (over y), stn: 4 (over z), chan: 4 (over x, core).
Axes of the slice: x: 2, y: 2, z: 4, core: 2. Of those that a mesh axis runs over, the one named last changes fastest.
Arguments:
- voltages: bfloat16 [256, 31, 8192], P(('grp', 'stn', 'chan')), parts along dimension 0, may hold values from -6 to 6
- taps: float32 [16, 8192], replicated, may hold values from -1.5 to 1.5
Outputs:
- visibilities: bfloat16 [8, 3, 256, 2, 1024], P(('grp', 'stn'), None, 'chan'), parts along dimension 0
There are 2 independent parts, one for each index of `grp`. A program takes and returns all parts, laid end to end along the dimension named above; an argument that names none is the same for every part. Nothing has to cross between parts.
All inputs are finite; a program needn't handle non-finite values.
Results may differ from a plain program's by a relative error of at most 0.0053.
Values may be sent and summed in bfloat16 or wider, within the bound.
A program may use at most 64 MiB of HBM per device.

v0:
```python
import functools
import math

import jax
import jax.numpy as jnp
import numpy as np
from jax import lax
from jax.experimental import pallas as pl
from jax.experimental.pallas import tpu as pltpu
from jax.sharding import PartitionSpec as P

AVG = 16


def from_behind(shard, axis, by):
    size = lax.axis_size(axis)
    return lax.ppermute(shard, axis, [(i, (i + by) % size) for i in range(size)])


def angle_table(rows, cols, modulus):
    product = (
        jnp.arange(rows, dtype=jnp.int32)[:, None]
        * jnp.arange(cols, dtype=jnp.int32)[None, :]
        % modulus
    )
    return 2.0 * math.pi / modulus * product.astype(jnp.float32)


def transform(weighted):
    rows_total = weighted.shape[0] * weighted.shape[1]
    frame_len = weighted.shape[2]
    inner = 128
    outer = frame_len // inner
    kept = frame_len // 2 // inner
    highest = lax.Precision.HIGHEST
    samples = weighted.reshape(rows_total, inner, outer)
    first = angle_table(inner, inner, inner)
    first_real = jnp.einsum("rqp,qk->rpk", samples, jnp.cos(first), precision=highest)
    first_imag = -jnp.einsum("rqp,qk->rpk", samples, jnp.sin(first), precision=highest)
    twist = angle_table(outer, inner, frame_len)
    twist_cos = jnp.cos(twist)
    twist_sin = jnp.sin(twist)
    second_real = first_real * twist_cos + first_imag * twist_sin
    second_imag = first_imag * twist_cos - first_real * twist_sin
    third = angle_table(outer, kept, outer)
    third_cos = jnp.cos(third)
    third_sin = jnp.sin(third)
    out_real = jnp.einsum("rpk,pm->rmk", second_real, third_cos, precision=highest) + jnp.einsum(
        "rpk,pm->rmk", second_imag, third_sin, precision=highest
    )
    out_imag = jnp.einsum("rpk,pm->rmk", second_imag, third_cos, precision=highest) - jnp.einsum(
        "rpk,pm->rmk", second_real, third_sin, precision=highest
    )
    scale = frame_len ** (-0.5)
    return (
        out_real.reshape(rows_total, kept * inner) * scale,
        out_imag.reshape(rows_total, kept * inner) * scale,
    )


def general(voltages, taps):
    inputs_here, frames, frame_len = voltages.shape
    tap_count = taps.shape[0]
    spectra_count = frames - tap_count + 1
    channels = frame_len // 2
    weighted = taps[0] * voltages[:, 0:spectra_count, :].astype(jnp.float32)
    for tap_index in range(1, tap_count):
        weighted = weighted + taps[tap_index] * voltages[
            :, tap_index : tap_index + spectra_count, :
        ].astype(jnp.float32)
    out_real, out_imag = transform(weighted)
    spectra = (
        jnp.stack([out_real, out_imag])
        .reshape(2, inputs_here, spectra_count, channels)
        .astype(jnp.bfloat16)
    )
    turned = lax.all_to_all(spectra, "chan", split_axis=3, concat_axis=1, tiled=True)
    block_inputs = turned.shape[1]
    chan_here = turned.shape[3]
    groups = chan_here // AVG
    scale = 1.0 / (spectra_count * AVG)
    half = lax.axis_size("stn") // 2
    reach = half + 1
    block = turned.reshape(2, block_inputs, spectra_count, groups, AVG)
    block = block.transpose(3, 0, 1, 2, 4).reshape(groups, 2 * block_inputs, spectra_count * AVG)

    def correlate(own, other):
        product = jnp.einsum("gak,gck->gac", own, other, preferred_element_type=jnp.float32)
        real_vis = (
            product[:, :block_inputs, :block_inputs] + product[:, block_inputs:, block_inputs:]
        )
        imag_vis = (
            product[:, block_inputs:, :block_inputs] - product[:, :block_inputs, block_inputs:]
        )
        both = jnp.stack([real_vis, imag_vis], axis=1).reshape(
            groups, 2, block_inputs * block_inputs
        )
        return (both * scale).astype(jnp.bfloat16)

    tiles = jnp.zeros((reach, groups, 2, block_inputs * block_inputs), jnp.bfloat16)
    tiles = tiles.at[0].set(correlate(block, block))

    def advance(distance, carry):
        moving, stack_now = carry
        moving = from_behind(moving, "stn", -1)
        stack_now = lax.dynamic_update_index_in_dim(
            stack_now, correlate(block, moving), distance, 0
        )
        return (moving, stack_now)

    moved, tiles = lax.fori_loop(1, reach, advance, (block, tiles))
    return tiles[None]


LANES = 128
SUB = 8
TILE = 16


def halves(table):
    high = table.astype(jnp.bfloat16)
    low = (table - high.astype(np.float64)).astype(jnp.bfloat16)
    return high, low


def fourier_tables(frame_len):
    outer = frame_len // LANES
    kept = frame_len // 2 // outer
    high_digit = np.arange(outer)
    lane = np.arange(LANES)
    first = 2.0 * np.pi / outer * (np.outer(high_digit, high_digit) % outer)
    first = np.concatenate([np.cos(first), -np.sin(first)], axis=0)
    high, low = halves(first)
    first = np.concatenate([high, low, high], axis=1)
    twist = 2.0 * np.pi / frame_len * (np.outer(high_digit, lane) % frame_len)
    last = 2.0 * np.pi / LANES * (np.outer(np.arange(kept), lane) % LANES)
    cos, sin = np.cos(last), np.sin(last)
    last = np.concatenate(
        [np.concatenate([cos, sin], axis=1), np.concatenate([-sin, cos], axis=1)], axis=0
    )
    high, low = halves(last * frame_len ** (-0.5))
    last = np.stack([high, low])
    return first, np.stack([np.cos(twist), np.sin(twist)]).astype(np.float32), last


def rows_by_rows(left, right):
    return lax.dot_general(
        left, right, (((1,), (1,)), ((), ())), preferred_element_type=jnp.float32
    )


def split(values):
    high = values.astype(jnp.bfloat16)
    return high, (values - high.astype(jnp.float32)).astype(jnp.bfloat16)


def spectra_kernel(v_ref, taps_ref, first_ref, twist_ref, last_ref, out_ref, frames, weighted, held):
    i = pl.program_id(0)
    tap_count = taps_ref.shape[0]
    frame_count = v_ref.shape[1]
    count = frame_count - tap_count + 1
    outer = v_ref.shape[2] // LANES
    kept = out_ref.shape[0]

    def filter_tile(tile, carry):
        lanes = pl.ds(pl.multiple_of(tile * LANES, LANES), LANES)
        frames[tile, 0:frame_count, :] = v_ref[0, :, lanes].astype(jnp.float32)
        total = taps_ref[0:1, lanes] * frames[tile, 0:count, :]
        for t in range(1, tap_count):
            total = total + taps_ref[t : t + 1, lanes] * frames[tile, t : t + count, :]
        weighted[pl.ds(tile, count, stride=outer), :] = total
        return carry

    lax.fori_loop(0, outer, filter_tile, 0, unroll=4)

    per_pass = 2 * LANES // outer
    for chunk in range(count // per_pass):
        parts = []
        for pair in range(per_pass // 2):
            s = chunk * per_pass + 2 * pair
            samples = jnp.concatenate(
                [weighted[s * outer : (s + 1) * outer, :], weighted[(s + 1) * outer : (s + 2) * outer, :]],
                axis=1,
            )
            high, low = split(samples)
            y = jnp.dot(
                first_ref[...],
                jnp.concatenate([high, high, low], axis=0),
                preferred_element_type=jnp.float32,
            )
            for k in range(2):
                real = y[:outer, k * LANES : (k + 1) * LANES]
                imag = y[outer:, k * LANES : (k + 1) * LANES]
                parts.append(
                    jnp.concatenate(
                        [
                            real * twist_ref[0] + imag * twist_ref[1],
                            imag * twist_ref[0] - real * twist_ref[1],
                        ],
                        axis=1,
                    )
                )
        high, low = split(jnp.concatenate(parts, axis=0))
        result = (
            rows_by_rows(last_ref[0], high)
            + rows_by_rows(last_ref[1], high)
            + rows_by_rows(last_ref[0], low)
        )
        for part in range(2):
            for k in range(2):
                held[chunk * 2 + k, pl.ds(part * SUB + i, kept, stride=TILE), :] = result[
                    part * kept : (part + 1) * kept, k * LANES : (k + 1) * LANES
                ]

    @pl.when(i == pl.num_programs(0) - 1)
    def _():
        for tile in range(held.shape[0]):
            out_ref[:, :, tile * LANES : (tile + 1) * LANES] = (
                held[tile].reshape(kept, TILE, LANES).astype(jnp.bfloat16)
            )


def local_spectra(voltages, taps):
    inputs_here, frame_count, frame_len = voltages.shape
    count = frame_count - taps.shape[0] + 1
    outer = frame_len // LANES
    kept = frame_len // 2 // outer
    tables = fourier_tables(frame_len)
    fixed = [taps] + [jnp.asarray(t) for t in tables]
    return pl.pallas_call(
        spectra_kernel,
        grid=(inputs_here,),
        in_specs=[pl.BlockSpec((1, frame_count, frame_len), lambda i: (i, 0, 0))]
        + [pl.BlockSpec(a.shape, lambda i, n=a.ndim: (0,) * n) for a in fixed],
        out_specs=pl.BlockSpec((kept, TILE, count * outer), lambda i: (0, 0, 0)),
        out_shape=jax.ShapeDtypeStruct((kept, TILE, count * outer), jnp.bfloat16),
        scratch_shapes=[
            pltpu.VMEM((outer, (frame_count + SUB - 1) // SUB * SUB, LANES), jnp.float32),
            pltpu.VMEM((count * outer, LANES), jnp.float32),
            pltpu.VMEM((count * outer // LANES, kept * TILE, LANES), jnp.float32),
        ],
        compiler_params=pltpu.CompilerParams(
            dimension_semantics=("arbitrary",), vmem_limit_bytes=48 * 2**20
        ),
    )(voltages, *fixed)


def correlate_kernel(
    n_stn, n_chan, count, spec_ref, mask_ref, out_ref, got, pair, mine,
    own_sem, send_sem, recv_sem, back_own, back_send, back_recv,
):
    grp = lax.axis_index("grp")
    stn = lax.axis_index("stn")
    chan = lax.axis_index("chan")
    reach = out_ref.shape[0]
    steps = got.shape[0]
    sub_groups = mask_ref.shape[0]
    block = TILE // 2 * n_chan
    across = LANES // block
    me = stn * n_chan + chan
    turns = [(a, b) for a in range(n_stn) for b in range(n_chan) if (a, b) != (0, 0)]

    def partner(turn):
        return lax.rem(stn + turn[0], n_stn), lax.rem(chan + turn[1], n_chan)

    def first_row(s, c):
        return (c * n_stn + s) * steps

    barrier = pltpu.get_barrier_semaphore()
    for turn in turns:
        s, c = partner(turn)
        pl.semaphore_signal(
            barrier, inc=1, device_id=(grp, s, c), device_id_type=pl.DeviceIdType.MESH
        )
    pl.semaphore_wait(barrier, len(turns))

    def own_copy(step):
        return pltpu.make_async_copy(
            spec_ref.at[first_row(stn, chan) + step], got.at[step, me], own_sem.at[step]
        )

    def outgoing(n, step):
        s, c = partner(turns[n])
        return pltpu.make_async_remote_copy(
            src_ref=spec_ref.at[first_row(s, c) + step],
            dst_ref=got.at[step, me],
            send_sem=send_sem.at[n, step],
            recv_sem=recv_sem.at[n, step],
            device_id=(grp, s, c),
            device_id_type=pl.DeviceIdType.MESH,
        )

    groups_here = steps * sub_groups

    def places(step):
        return pl.ds(step * sub_groups, sub_groups), pl.ds(
            stn * groups_here + step * sub_groups, sub_groups
        )

    def back_own_copy(step):
        src, dst = places(step)
        return pltpu.make_async_copy(mine.at[stn, :, src], out_ref.at[:, dst], back_own.at[step])

    def going_back(n, step):
        src, dst = places(step)
        s = lax.rem(stn + n, n_stn)
        return pltpu.make_async_remote_copy(
            src_ref=mine.at[s, :, src],
            dst_ref=out_ref.at[:, dst],
            send_sem=back_send.at[n - 1, step],
            recv_sem=back_recv.at[n - 1, step],
            device_id=(grp, s, chan),
            device_id_type=pl.DeviceIdType.MESH,
        )

    order = sorted(range(len(turns)), key=lambda n: -turns[n][0] % n_stn == 0)
    for step in range(steps):
        own_copy(step).start()
        for n in order:
            outgoing(n, step).start()

    scale = 1.0 / (count * AVG)
    n_rows = n_stn * n_chan * SUB
    lane_part = lax.broadcasted_iota(jnp.int32, (SUB, LANES), 1) // block

    def one_step(step, carry):
        own_copy(step).wait()
        for n in range(len(turns)):
            outgoing(n, step).wait_recv()
        both = got[step].astype(jnp.float32)
        width = both.shape[2]
        rows = jnp.concatenate(
            [both[:, :SUB, :].reshape(n_rows, width), both[:, SUB:, :].reshape(n_rows, width)], axis=0
        ).astype(jnp.bfloat16)
        for g in range(sub_groups):
            chosen = rows.reshape(2 * n_rows // TILE, TILE, width) * mask_ref[g][None]
            product = rows_by_rows(chosen.reshape(2 * n_rows, width), rows)
            pair[g, 0] = (product[:n_rows, :n_rows] + product[n_rows:, n_rows:]) * scale
            pair[g, 1] = (product[n_rows:, :n_rows] - product[:n_rows, n_rows:]) * scale
            for b in range(n_stn):
                slabs = [
                    [pair[g, part, pl.ds(b * block + e, SUB, stride=across), :] for e in range(across)]
                    for part in range(2)
                ]
                for d in range(reach):
                    other = (b + d) % n_stn
                    tiles = []
                    for part in range(2):
                        flat = None
                        for e in range(across):
                            shift = (e - other) % across * block
                            moved = pltpu.roll(slabs[part][e], shift, 1) if shift else slabs[part][e]
                            flat = moved if flat is None else jnp.where(lane_part == e, moved, flat)
                        tiles.append(flat)
                    mine[b, d, step * sub_groups + g] = jnp.concatenate(tiles, axis=0).astype(
                        jnp.bfloat16
                    )
        back_own_copy(step).start()
        for n in range(1, n_stn):
            going_back(n, step).start()
        return carry

    lax.fori_loop(0, steps, one_step, 0)

    for step in range(steps):
        back_own_copy(step).wait()
        for n in range(len(turns)):
            outgoing(n, step).wait_send()
        for n in range(1, n_stn):
            going_back(n, step).wait()


def correlate_all(spectra, n_stn, n_chan, count):
    kept, tile, width = spectra.shape
    outer = width // count
    steps = kept // (n_stn * n_chan)
    sub_groups = outer // AVG
    reach = n_stn // 2 + 1
    peers = n_stn * n_chan - 1
    groups = kept // n_chan * sub_groups
    mask = (np.arange(width) % outer // AVG)[None, :] == np.arange(sub_groups)[:, None]
    mask = jnp.asarray(
        np.broadcast_to(mask[:, None, :], (sub_groups, TILE, width)).astype(jnp.bfloat16)
    )
    vmem = pl.BlockSpec(memory_space=pltpu.VMEM)
    return pl.pallas_call(
        functools.partial(correlate_kernel, n_stn, n_chan, count),
        in_specs=[vmem, vmem],
        out_specs=vmem,
        out_shape=jax.ShapeDtypeStruct((reach, groups, TILE, LANES), jnp.bfloat16),
        scratch_shapes=[
            pltpu.VMEM((steps, n_stn * n_chan, TILE, width), jnp.bfloat16),
            pltpu.VMEM((sub_groups, 2, LANES, LANES), jnp.float32),
            pltpu.VMEM((n_stn, reach, steps * sub_groups, TILE, LANES), jnp.bfloat16),
            pltpu.SemaphoreType.DMA((steps,)),
            pltpu.SemaphoreType.DMA((peers, steps)),
            pltpu.SemaphoreType.DMA((peers, steps)),
            pltpu.SemaphoreType.DMA((steps,)),
            pltpu.SemaphoreType.DMA((n_stn - 1, steps)),
            pltpu.SemaphoreType.DMA((n_stn - 1, steps)),
        ],
        compiler_params=pltpu.CompilerParams(
            collective_id=0, has_side_effects=True, vmem_limit_bytes=48 * 2**20
        ),
    )(spectra, mask)


def local(voltages, taps):
    inputs_here, frame_count, frame_len = voltages.shape
    count = frame_count - taps.shape[0] + 1
    n_stn, n_chan = lax.axis_size("stn"), lax.axis_size("chan")
    outer = frame_len // LANES
    fits = (
        inputs_here == SUB
        and inputs_here * n_stn * n_chan == LANES
        and frame_len % (LANES * AVG) == 0
        and LANES % outer == 0
        and count % (2 * LANES // outer) == 0
        and count % TILE == 0
        and frame_len // 2 // outer % (n_stn * n_chan) == 0
        and (inputs_here * n_chan) ** 2 == SUB * LANES
    )
    if not fits:
        return general(voltages, taps)
    tiles = correlate_all(local_spectra(voltages, taps), n_stn, n_chan, count)
    reach, groups = tiles.shape[:2]
    return tiles.reshape(1, reach, groups, 2, (inputs_here * n_chan) ** 2)


def solution(mesh):
    placed = (P(("grp", "stn", "chan"), None, None), P())
    return jax.shard_map(
        local,
        mesh=mesh,
        in_specs=placed,
        out_specs=P(("grp", "stn"), None, "chan", None, None),
        check_vma=False,
    )
```

profile of v0, /device:TPU:0, one launch (start us, length us, event | category | flops | bytes accessed | tf_op | source)
XLA Modules:
  0.0 99.0 jit_solution(2875287851787121014)
XLA Ops:
  0.0 0.0 copy-start.1
  0.0 0.0 copy-start.3
  0.0 0.0 copy-start.4
  0.0 0.0 copy-start
  0.0 6.4 %copy.7.v_ref = bf16[8,31,8192]{2,1,0:T(8,128)(2,1)} copy(bf16[8,31,8192]{2,0,1:T(8,128)(2,1)} %param.6) | data formatting | bytes 8126464 | tf_op args[0]
  6.4 0.0 copy-done.1
  6.4 0.0 copy-done.3
  6.4 0.0 copy-done.4
  6.4 0.0 copy-done
  6.4 0.0 copy-start.2
  6.4 21.5 %shard_map.64.spec_ref = bf16[64,16,1024]{2,1,0:T(8,128)(2,1)S(1)} custom-call(bf16[8,31,8192]{2,1,0:T(8,128)(2,1)} %copy.7.v_ref, f32[16,8192]{1,0:T(8,128)S(1)} %copy-done, bf16[128,192]{1,0:T(8,128)(2,1)S(1)} %copy-done.4, f32[2,64,128]{2,1,0:T(8,128)S(1)} %copy-done.3, bf16[2,128,256]{2,1,0:T(8,128)(2,1)S(1)} %copy-done.1), custom_call_target="tpu_custom_call" | custom-call | tf_op jit(solution)/shard_map/pallas_call | solution.py:230
  27.9 0.0 copy-done.2
  27.9 70.0 %shard_map.65 = bf16[3,64,16,128]{3,2,1,0:T(8,128)(2,1)S(1)} custom-call(bf16[64,16,1024]{2,1,0:T(8,128)(2,1)S(1)} %shard_map.64.spec_ref, bf16[4,16,1024]{2,1,0:T(8,128)(2,1)S(1)} %copy-done.2), custom_call_target="tpu_custom_call" | custom-call | tf_op jit(solution)/shard_map/pallas_call | solution.py:386
  97.9 1.1 %reshape.3 = bf16[1,3,64,2,1024]{4,3,2,1,0:T(2,128)(2,1)} reshape(bf16[3,64,16,128]{3,2,1,0:T(8,128)(2,1)S(1)} %shard_map.65) | data formatting | bytes 1572864 | tf_op jit(solution)/shard_map/reshape | solution.py:427
Async XLA Ops:
  0.0 6.4 %copy-start.1 = (bf16[2,128,256]{2,1,0:T(8,128)(2,1)S(1)}, bf16[2,128,256]{2,1,0:T(8,128)(2,1)}, u32[]{:S(2)}) copy-start(bf16[2,128,256]{2,1,0:T(8,128)(2,1)} %constant.10.clone.last_ref) | copy-start | bytes 393220
  0.0 6.4 %copy-start.3 = (f32[2,64,128]{2,1,0:T(8,128)S(1)}, f32[2,64,128]{2,1,0:T(8,128)}, u32[]{:S(2)}) copy-start(f32[2,64,128]{2,1,0:T(8,128)} %constant.9.clone.twist_ref) | copy-start | bytes 196612
  0.0 6.4 %copy-start.4 = (bf16[128,192]{1,0:T(8,128)(2,1)S(1)}, bf16[128,192]{1,0:T(8,128)(2,1)}, u32[]{:S(2)}) copy-start(bf16[128,192]{1,0:T(8,128)(2,1)} %constant.8.clone.first_ref) | copy-start | bytes 147460
  0.0 6.4 %copy-start = (f32[16,8192]{1,0:T(8,128)S(1)}, f32[16,8192]{1,0:T(8,128)}, u32[]{:S(2)}) copy-start(f32[16,8192]{1,0:T(8,128)} %taps_ref.1) | copy-start | bytes 1572868
  6.4 21.5 %copy-start.2 = (bf16[4,16,1024]{2,1,0:T(8,128)(2,1)S(1)}, bf16[4,16,1024]{2,1,0:T(8,128)(2,1)}, u32[]{:S(2)}) copy-start(bf16[4,16,1024]{2,1,0:T(8,128)(2,1)} %constant.11.clone.mask_ref) | copy-start | bytes 393220
where the time goes:
time: 99.1 us; the launch traced here: 99 us
  Pallas kernels  91.4 us (92%)
  local copies, waits for them, and re-layouts  7.47 us (8%)
    pallas_call x1, Pallas kernels, correlate_all(): pl.pallas_call(functools.partial(correlate_kernel, n_stn, n_chan, count),...  70 us
    pallas_call x1, Pallas kernels, local_spectra(): pl.pallas_call(spectra_kernel, grid=(inputs_here,), in_specs=[pl.BlockSpe...  21.5 us
    unnamed x11, local copies, waits for them, and re-layouts  6.41 us

commit v1 on v0

--- a/solution.py
+++ b/solution.py
@@ -154,106 +154,21 @@
     return high, (values - high.astype(jnp.float32)).astype(jnp.bfloat16)
 
 
-def spectra_kernel(v_ref, taps_ref, first_ref, twist_ref, last_ref, out_ref, frames, weighted, held):
-    i = pl.program_id(0)
-    tap_count = taps_ref.shape[0]
-    frame_count = v_ref.shape[1]
-    count = frame_count - tap_count + 1
-    outer = v_ref.shape[2] // LANES
-    kept = out_ref.shape[0]
-
-    def filter_tile(tile, carry):
-        lanes = pl.ds(pl.multiple_of(tile * LANES, LANES), LANES)
-        frames[tile, 0:frame_count, :] = v_ref[0, :, lanes].astype(jnp.float32)
-        total = taps_ref[0:1, lanes] * frames[tile, 0:count, :]
-        for t in range(1, tap_count):
-            total = total + taps_ref[t : t + 1, lanes] * frames[tile, t : t + count, :]
-        weighted[pl.ds(tile, count, stride=outer), :] = total
-        return carry
-
-    lax.fori_loop(0, outer, filter_tile, 0, unroll=4)
-
-    per_pass = 2 * LANES // outer
-    for chunk in range(count // per_pass):
-        parts = []
-        for pair in range(per_pass // 2):
-            s = chunk * per_pass + 2 * pair
-            samples = jnp.concatenate(
-                [weighted[s * outer : (s + 1) * outer, :], weighted[(s + 1) * outer : (s + 2) * outer, :]],
-                axis=1,
-            )
-            high, low = split(samples)
-            y = jnp.dot(
-                first_ref[...],
-                jnp.concatenate([high, high, low], axis=0),
-                preferred_element_type=jnp.float32,
-            )
-            for k in range(2):
-                real = y[:outer, k * LANES : (k + 1) * LANES]
-                imag = y[outer:, k * LANES : (k + 1) * LANES]
-                parts.append(
-                    jnp.concatenate(
-                        [
-                            real * twist_ref[0] + imag * twist_ref[1],
-                            imag * twist_ref[0] - real * twist_ref[1],
-                        ],
-                        axis=1,
-                    )
-                )
-        high, low = split(jnp.concatenate(parts, axis=0))
-        result = (
-            rows_by_rows(last_ref[0], high)
-            + rows_by_rows(last_ref[1], high)
-            + rows_by_rows(last_ref[0], low)
-        )
-        for part in range(2):
-            for k in range(2):
-                held[chunk * 2 + k, pl.ds(part * SUB + i, kept, stride=TILE), :] = result[
-                    part * kept : (part + 1) * kept, k * LANES : (k + 1) * LANES
-                ]
-
-    @pl.when(i == pl.num_programs(0) - 1)
-    def _():
-        for tile in range(held.shape[0]):
-            out_ref[:, :, tile * LANES : (tile + 1) * LANES] = (
-                held[tile].reshape(kept, TILE, LANES).astype(jnp.bfloat16)
-            )
-
-
-def local_spectra(voltages, taps):
-    inputs_here, frame_count, frame_len = voltages.shape
-    count = frame_count - taps.shape[0] + 1
-    outer = frame_len // LANES
-    kept = frame_len // 2 // outer
-    tables = fourier_tables(frame_len)
-    fixed = [taps] + [jnp.asarray(t) for t in tables]
-    return pl.pallas_call(
-        spectra_kernel,
-        grid=(inputs_here,),
-        in_specs=[pl.BlockSpec((1, frame_count, frame_len), lambda i: (i, 0, 0))]
-        + [pl.BlockSpec(a.shape, lambda i, n=a.ndim: (0,) * n) for a in fixed],
-        out_specs=pl.BlockSpec((kept, TILE, count * outer), lambda i: (0, 0, 0)),
-        out_shape=jax.ShapeDtypeStruct((kept, TILE, count * outer), jnp.bfloat16),
-        scratch_shapes=[
-            pltpu.VMEM((outer, (frame_count + SUB - 1) // SUB * SUB, LANES), jnp.float32),
-            pltpu.VMEM((count * outer, LANES), jnp.float32),
-            pltpu.VMEM((count * outer // LANES, kept * TILE, LANES), jnp.float32),
-        ],
-        compiler_params=pltpu.CompilerParams(
-            dimension_semantics=("arbitrary",), vmem_limit_bytes=48 * 2**20
-        ),
-    )(voltages, *fixed)
-
-
-def correlate_kernel(
-    n_stn, n_chan, count, spec_ref, mask_ref, out_ref, got, pair, mine,
+def fused_kernel(
+    n_stn, n_chan, v_ref, taps_ref, first_ref, twist_ref, last_ref, mask_ref, out_ref,
+    weighted, held, spec, got, pair, mine,
     own_sem, send_sem, recv_sem, back_own, back_send, back_recv,
 ):
     grp = lax.axis_index("grp")
     stn = lax.axis_index("stn")
     chan = lax.axis_index("chan")
     reach = out_ref.shape[0]
-    steps = got.shape[0]
+    chunks, _, steps, _, width = got.shape
+    outer = v_ref.shape[2] // LANES
+    kept = spec.shape[1]
+    tap_count = taps_ref.shape[0]
+    count = v_ref.shape[0] - tap_count + 1
+    per_chunk = count // chunks
     sub_groups = mask_ref.shape[0]
     block = TILE // 2 * n_chan
     across = LANES // block
@@ -274,18 +189,18 @@
         )
     pl.semaphore_wait(barrier, len(turns))
 
-    def own_copy(step):
+    def own_copy(chunk):
         return pltpu.make_async_copy(
-            spec_ref.at[first_row(stn, chan) + step], got.at[step, me], own_sem.at[step]
-        )
-
-    def outgoing(n, step):
+            spec.at[chunk, pl.ds(first_row(stn, chan), steps)], got.at[chunk, me], own_sem.at[chunk]
+        )
+
+    def outgoing(n, chunk):
         s, c = partner(turns[n])
         return pltpu.make_async_remote_copy(
-            src_ref=spec_ref.at[first_row(s, c) + step],
-            dst_ref=got.at[step, me],
-            send_sem=send_sem.at[n, step],
-            recv_sem=recv_sem.at[n, step],
+            src_ref=spec.at[chunk, pl.ds(first_row(s, c), steps)],
+            dst_ref=got.at[chunk, me],
+            send_sem=send_sem.at[n, chunk],
+            recv_sem=recv_sem.at[n, chunk],
             device_id=(grp, s, c),
             device_id_type=pl.DeviceIdType.MESH,
         )
@@ -313,28 +228,104 @@
             device_id_type=pl.DeviceIdType.MESH,
         )
 
-    order = sorted(range(len(turns)), key=lambda n: -turns[n][0] % n_stn == 0)
-    for step in range(steps):
-        own_copy(step).start()
+    order = sorted(range(len(turns)), key=lambda n: turns[n][0] == 0)
+
+    def one_chunk(chunk, carry):
+        def filter_tile(tile, inner):
+            lanes = pl.ds(pl.multiple_of(tile * LANES, LANES), LANES)
+            frames = [
+                v_ref[chunk * per_chunk + t, :, lanes].astype(jnp.float32)
+                for t in range(per_chunk + tap_count - 1)
+            ]
+            totals = [None] * per_chunk
+            for t in range(tap_count):
+                tap = jnp.broadcast_to(taps_ref[t : t + 1, lanes], (SUB, LANES))
+                for s in range(per_chunk):
+                    term = tap * frames[s + t]
+                    totals[s] = term if t == 0 else totals[s] + term
+            for s in range(per_chunk):
+                weighted[pl.ds(s * SUB * outer + tile, SUB, stride=outer), :] = totals[s]
+            return inner
+
+        lax.fori_loop(0, outer, filter_tile, 0, unroll=2)
+
+        def one_input(i, inner):
+            parts = []
+            for s in range(0, per_chunk, 2):
+                samples = jnp.concatenate(
+                    [
+                        weighted[pl.ds(pl.multiple_of(((s + k) * SUB + i) * outer, outer), outer), :]
+                        for k in range(2)
+                    ],
+                    axis=1,
+                )
+                high, low = split(samples)
+                y = jnp.dot(
+                    first_ref[...],
+                    jnp.concatenate([high, high, low], axis=0),
+                    preferred_element_type=jnp.float32,
+                )
+                for k in range(2):
+                    real = y[:outer, k * LANES : (k + 1) * LANES]
+                    imag = y[outer:, k * LANES : (k + 1) * LANES]
+                    parts.append(
+                        jnp.concatenate(
+                            [
+                                real * twist_ref[0] + imag * twist_ref[1],
+                                imag * twist_ref[0] - real * twist_ref[1],
+                            ],
+                            axis=1,
+                        )
+                    )
+            high, low = split(jnp.concatenate(parts, axis=0))
+            result = (
+                rows_by_rows(last_ref[0], high)
+                + rows_by_rows(last_ref[1], high)
+                + rows_by_rows(last_ref[0], low)
+            )
+            for part in range(2):
+                for k in range(width // LANES):
+                    held[k, pl.ds(part * SUB + i, kept, stride=TILE), :] = result[
+                        part * kept : (part + 1) * kept, k * LANES : (k + 1) * LANES
+                    ]
+            return inner
+
+        lax.fori_loop(0, SUB, one_input, 0, unroll=2)
+        for k in range(width // LANES):
+            spec[chunk, :, :, k * LANES : (k + 1) * LANES] = (
+                held[k].reshape(kept, TILE, LANES).astype(jnp.bfloat16)
+            )
+        own_copy(chunk).start()
         for n in order:
-            outgoing(n, step).start()
+            outgoing(n, chunk).start()
+        return carry
+
+    lax.fori_loop(0, chunks, one_chunk, 0)
+
+    for chunk in range(chunks):
+        own_copy(chunk).wait()
+        for n in range(len(turns)):
+            outgoing(n, chunk).wait_recv()
 
     scale = 1.0 / (count * AVG)
     n_rows = n_stn * n_chan * SUB
     lane_part = lax.broadcasted_iota(jnp.int32, (SUB, LANES), 1) // block
 
     def one_step(step, carry):
-        own_copy(step).wait()
-        for n in range(len(turns)):
-            outgoing(n, step).wait_recv()
-        both = got[step].astype(jnp.float32)
-        width = both.shape[2]
-        rows = jnp.concatenate(
-            [both[:, :SUB, :].reshape(n_rows, width), both[:, SUB:, :].reshape(n_rows, width)], axis=0
-        ).astype(jnp.bfloat16)
+        columns = []
+        for chunk in range(chunks):
+            both = got[chunk, :, step].astype(jnp.float32)
+            columns.append(
+                jnp.concatenate(
+                    [both[:, :SUB, :].reshape(n_rows, width), both[:, SUB:, :].reshape(n_rows, width)],
+                    axis=0,
+                ).astype(jnp.bfloat16)
+            )
+        rows = jnp.concatenate(columns, axis=1)
+        total = chunks * width
         for g in range(sub_groups):
-            chosen = rows.reshape(2 * n_rows // TILE, TILE, width) * mask_ref[g][None]
-            product = rows_by_rows(chosen.reshape(2 * n_rows, width), rows)
+            chosen = rows.reshape(2 * n_rows // TILE, TILE, total) * mask_ref[g][None]
+            product = rows_by_rows(chosen.reshape(2 * n_rows, total), rows)
             pair[g, 0] = (product[:n_rows, :n_rows] + product[n_rows:, n_rows:]) * scale
             pair[g, 1] = (product[n_rows:, :n_rows] - product[:n_rows, n_rows:]) * scale
             for b in range(n_stn):
@@ -362,39 +353,47 @@
 
     lax.fori_loop(0, steps, one_step, 0)
 
+    for chunk in range(chunks):
+        for n in range(len(turns)):
+            outgoing(n, chunk).wait_send()
     for step in range(steps):
         back_own_copy(step).wait()
-        for n in range(len(turns)):
-            outgoing(n, step).wait_send()
         for n in range(1, n_stn):
             going_back(n, step).wait()
 
 
-def correlate_all(spectra, n_stn, n_chan, count):
-    kept, tile, width = spectra.shape
-    outer = width // count
+def fused(voltages, taps, n_stn, n_chan):
+    inputs_here, frame_count, frame_len = voltages.shape
+    count = frame_count - taps.shape[0] + 1
+    outer = frame_len // LANES
+    kept = frame_len // 2 // outer
+    per_chunk = 2 * LANES // outer
+    chunks = count // per_chunk
+    width = per_chunk * outer
+    peers = n_stn * n_chan - 1
     steps = kept // (n_stn * n_chan)
     sub_groups = outer // AVG
     reach = n_stn // 2 + 1
-    peers = n_stn * n_chan - 1
     groups = kept // n_chan * sub_groups
-    mask = (np.arange(width) % outer // AVG)[None, :] == np.arange(sub_groups)[:, None]
-    mask = jnp.asarray(
-        np.broadcast_to(mask[:, None, :], (sub_groups, TILE, width)).astype(jnp.bfloat16)
-    )
+    mask = (np.arange(count * outer) % outer // AVG)[None, :] == np.arange(sub_groups)[:, None]
+    mask = np.broadcast_to(mask[:, None, :], (sub_groups, TILE, count * outer)).astype(jnp.bfloat16)
+    tables = [jnp.asarray(t) for t in (*fourier_tables(frame_len), mask)]
     vmem = pl.BlockSpec(memory_space=pltpu.VMEM)
     return pl.pallas_call(
-        functools.partial(correlate_kernel, n_stn, n_chan, count),
-        in_specs=[vmem, vmem],
+        functools.partial(fused_kernel, n_stn, n_chan),
+        in_specs=[vmem] * 6,
         out_specs=vmem,
         out_shape=jax.ShapeDtypeStruct((reach, groups, TILE, LANES), jnp.bfloat16),
         scratch_shapes=[
-            pltpu.VMEM((steps, n_stn * n_chan, TILE, width), jnp.bfloat16),
+            pltpu.VMEM((per_chunk * inputs_here * outer, LANES), jnp.float32),
+            pltpu.VMEM((width // LANES, kept * TILE, LANES), jnp.float32),
+            pltpu.VMEM((chunks, kept, TILE, width), jnp.bfloat16),
+            pltpu.VMEM((chunks, n_stn * n_chan, steps, TILE, width), jnp.bfloat16),
             pltpu.VMEM((sub_groups, 2, LANES, LANES), jnp.float32),
             pltpu.VMEM((n_stn, reach, steps * sub_groups, TILE, LANES), jnp.bfloat16),
-            pltpu.SemaphoreType.DMA((steps,)),
-            pltpu.SemaphoreType.DMA((peers, steps)),
-            pltpu.SemaphoreType.DMA((peers, steps)),
+            pltpu.SemaphoreType.DMA((chunks,)),
+            pltpu.SemaphoreType.DMA((peers, chunks)),
+            pltpu.SemaphoreType.DMA((peers, chunks)),
             pltpu.SemaphoreType.DMA((steps,)),
             pltpu.SemaphoreType.DMA((n_stn - 1, steps)),
             pltpu.SemaphoreType.DMA((n_stn - 1, steps)),
@@ -402,7 +401,7 @@
         compiler_params=pltpu.CompilerParams(
             collective_id=0, has_side_effects=True, vmem_limit_bytes=48 * 2**20
         ),
-    )(spectra, mask)
+    )(jnp.transpose(voltages, (1, 0, 2)), taps, *tables)
 
 
 def local(voltages, taps):
@@ -422,7 +421,7 @@
     )
     if not fits:
         return general(voltages, taps)
-    tiles = correlate_all(local_spectra(voltages, taps), n_stn, n_chan, count)
+    tiles = fused(voltages, taps, n_stn, n_chan)
     reach, groups = tiles.shape[:2]
     return tiles.reshape(1, reach, groups, 2, (inputs_here * n_chan) ** 2)
 

time: 99.1 us -> 83.2 us (0.84)
  Pallas kernels: 91.4 us -> 75.1 us
    pallas_call x2 -> x1, Pallas kernels: 91.4 us -> 75.1 us  [fused(): pl.pallas_call(functools.partial(fused_kernel, n_stn, n_chan), in_specs=[...]
    unnamed x11 -> x12, local copies, waits for them, and re-layouts: 6.41 us -> 6.68 us
where the time goes in v1:
time: 83.2 us; the launch traced here: 82.9 us
  Pallas kernels  75.1 us (90%)
  local copies, waits for them, and re-layouts  7.74 us (9%)
    pallas_call x1, Pallas kernels, fused(): pl.pallas_call(functools.partial(fused_kernel, n_stn, n_chan), in_specs=[...  75.1 us
    unnamed x12, local copies, waits for them, and re-layouts  6.68 us

profile of v1, /device:TPU:0, one launch (start us, length us, event | category | flops | bytes accessed | tf_op | source)
XLA Modules:
  0.0 82.9 jit_solution(18422312200310244132)
XLA Ops:
  0.0 0.0 copy-start
  0.0 2.1 %copy-done = bf16[8,31,8192]{2,0,1:T(8,128)(2,1)S(1)} copy-done((bf16[8,31,8192]{2,0,1:T(8,128)(2,1)S(1)}, bf16[8,31,8192]{2,0,1:T(8,128)(2,1)}, u32[]{:S(2)}) %copy-start) | copy-done | bytes 4063256
  2.2 0.0 copy-start.1
  2.2 1.0 %copy-done.1 = f32[16,8192]{1,0:T(8,128)S(1)} copy-done((f32[16,8192]{1,0:T(8,128)S(1)}, f32[16,8192]{1,0:T(8,128)}, u32[]{:S(2)}) %copy-start.1) | copy-done | bytes 524312
  3.2 0.0 copy-start.2
  3.2 0.9 %copy-done.2 = bf16[4,16,1024]{2,1,0:T(8,128)(2,1)S(1)} copy-done((bf16[4,16,1024]{2,1,0:T(8,128)(2,1)S(1)}, bf16[4,16,1024]{2,1,0:T(8,128)(2,1)}, u32[]{:S(2)}) %copy-start.2) | copy-done | bytes 131096
  4.1 0.0 copy-start.3
  4.1 0.9 %copy-done.3 = bf16[2,128,256]{2,1,0:T(8,128)(2,1)S(1)} copy-done((bf16[2,128,256]{2,1,0:T(8,128)(2,1)S(1)}, bf16[2,128,256]{2,1,0:T(8,128)(2,1)}, u32[]{:S(2)}) %copy-start.3) | copy-done | bytes 131096
  5.0 0.0 copy-start.4
  5.0 0.8 %copy-done.4 = f32[2,64,128]{2,1,0:T(8,128)S(1)} copy-done((f32[2,64,128]{2,1,0:T(8,128)S(1)}, f32[2,64,128]{2,1,0:T(8,128)}, u32[]{:S(2)}) %copy-start.4) | copy-done | bytes 65560
  5.8 0.0 copy-start.5
  5.8 0.8 %copy-done.5 = bf16[128,192]{1,0:T(8,128)(2,1)S(1)} copy-done((bf16[128,192]{1,0:T(8,128)(2,1)S(1)}, bf16[128,192]{1,0:T(8,128)(2,1)}, u32[]{:S(2)}) %copy-start.5) | copy-done | bytes 49176
  6.7 75.1 %shard_map.64 = bf16[3,64,16,128]{3,2,1,0:T(8,128)(2,1)S(1)} custom-call(bf16[31,8,8192]{2,1,0:T(8,128)(2,1)S(1)} %bitcast.3, f32[16,8192]{1,0:T(8,128)S(1)} %copy-done.1, bf16[128,192]{1,0:T(8,128)(2,1)S(1)} %copy-done.5, f32[2,64,128]{2,1,0:T(8,128)S(1)} %copy-done.4, bf16[2,128,256]{2,1,0:T(8,128)(2,1)S(1)} %copy-done.3, bf16[4,16,1024]{2,1,0:T(8,128)(2,1)S(1)} %copy-done.2), custom_call_target="tpu_custom_call" | custom-call | tf_op jit(solution)/shard_map/pallas_call | solution.py:382
  81.8 1.1 %reshape.3 = bf16[1,3,64,2,1024]{4,3,2,1,0:T(2,128)(2,1)} reshape(bf16[3,64,16,128]{3,2,1,0:T(8,128)(2,1)S(1)} %shard_map.64) | data formatting | bytes 1572864 | tf_op jit(solution)/shard_map/reshape | solution.py:426
Async XLA Ops:
  0.0 2.2 %copy-start = (bf16[8,31,8192]{2,0,1:T(8,128)(2,1)S(1)}, bf16[8,31,8192]{2,0,1:T(8,128)(2,1)}, u32[]{:S(2)}) copy-start(bf16[8,31,8192]{2,0,1:T(8,128)(2,1)} %param.6) | copy-start | bytes 12189700
  2.2 1.0 %copy-start.1 = (f32[16,8192]{1,0:T(8,128)S(1)}, f32[16,8192]{1,0:T(8,128)}, u32[]{:S(2)}) copy-start(f32[16,8192]{1,0:T(8,128)} %taps_ref.1) | copy-start | bytes 1572868
  3.2 0.9 %copy-start.2 = (bf16[4,16,1024]{2,1,0:T(8,128)(2,1)S(1)}, bf16[4,16,1024]{2,1,0:T(8,128)(2,1)}, u32[]{:S(2)}) copy-start(bf16[4,16,1024]{2,1,0:T(8,128)(2,1)} %constant.11.clone.mask_ref) | copy-start | bytes 393220
  4.1 0.9 %copy-start.3 = (bf16[2,128,256]{2,1,0:T(8,128)(2,1)S(1)}, bf16[2,128,256]{2,1,0:T(8,128)(2,1)}, u32[]{:S(2)}) copy-start(bf16[2,128,256]{2,1,0:T(8,128)(2,1)} %constant.10.clone.last_ref) | copy-start | bytes 393220
  5.0 0.8 %copy-start.4 = (f32[2,64,128]{2,1,0:T(8,128)S(1)}, f32[2,64,128]{2,1,0:T(8,128)}, u32[]{:S(2)}) copy-start(f32[2,64,128]{2,1,0:T(8,128)} %constant.9.clone.twist_ref) | copy-start | bytes 196612
  5.8 0.8 %copy-start.5 = (bf16[128,192]{1,0:T(8,128)(2,1)S(1)}, bf16[128,192]{1,0:T(8,128)(2,1)}, u32[]{:S(2)}) copy-start(bf16[128,192]{1,0:T(8,128)(2,1)} %constant.8.clone.first_ref) | copy-start | bytes 147460

commit v2 on v1

--- a/solution.py
+++ b/solution.py
@@ -155,8 +155,8 @@
 
 
 def fused_kernel(
-    n_stn, n_chan, v_ref, taps_ref, first_ref, twist_ref, last_ref, mask_ref, out_ref,
-    weighted, held, spec, got, pair, mine,
+    n_stn, n_chan, v_hbm, taps_hbm, first_hbm, twist_hbm, last_hbm, mask_hbm, out_ref,
+    v_ref, taps_ref, first_ref, twist_ref, last_ref, mask_ref, in_sem, weighted, held, spec, got, pair, mine,
     own_sem, send_sem, recv_sem, back_own, back_send, back_recv,
 ):
     grp = lax.axis_index("grp")
@@ -181,6 +181,20 @@
     def first_row(s, c):
         return (c * n_stn + s) * steps
 
+    ahead = per_chunk + tap_count - 1
+    loads = [
+        pltpu.make_async_copy(v_hbm.at[pl.ds(0, ahead)], v_ref.at[pl.ds(0, ahead)], in_sem.at[0]),
+        pltpu.make_async_copy(taps_hbm, taps_ref, in_sem.at[1]),
+        pltpu.make_async_copy(first_hbm, first_ref, in_sem.at[2]),
+        pltpu.make_async_copy(twist_hbm, twist_ref, in_sem.at[3]),
+        pltpu.make_async_copy(last_hbm, last_ref, in_sem.at[4]),
+    ]
+    rest = pl.ds(ahead, v_ref.shape[0] - ahead)
+    later = pltpu.make_async_copy(v_hbm.at[rest], v_ref.at[rest], in_sem.at[5])
+    last_load = pltpu.make_async_copy(mask_hbm, mask_ref, in_sem.at[6])
+    for copy in [*loads, later, last_load]:
+        copy.start()
+
     barrier = pltpu.get_barrier_semaphore()
     for turn in turns:
         s, c = partner(turn)
@@ -231,6 +245,10 @@
     order = sorted(range(len(turns)), key=lambda n: turns[n][0] == 0)
 
     def one_chunk(chunk, carry):
+        @pl.when(chunk == 1)
+        def _():
+            later.wait()
+
         def filter_tile(tile, inner):
             lanes = pl.ds(pl.multiple_of(tile * LANES, LANES), LANES)
             frames = [
@@ -300,7 +318,10 @@
             outgoing(n, chunk).start()
         return carry
 
+    for copy in loads:
+        copy.wait()
     lax.fori_loop(0, chunks, one_chunk, 0)
+    last_load.wait()
 
     for chunk in range(chunks):
         own_copy(chunk).wait()
@@ -378,13 +399,16 @@
     mask = (np.arange(count * outer) % outer // AVG)[None, :] == np.arange(sub_groups)[:, None]
     mask = np.broadcast_to(mask[:, None, :], (sub_groups, TILE, count * outer)).astype(jnp.bfloat16)
     tables = [jnp.asarray(t) for t in (*fourier_tables(frame_len), mask)]
+    frames_first = jnp.transpose(voltages, (1, 0, 2))
     vmem = pl.BlockSpec(memory_space=pltpu.VMEM)
     return pl.pallas_call(
         functools.partial(fused_kernel, n_stn, n_chan),
-        in_specs=[vmem] * 6,
+        in_specs=[pl.BlockSpec(memory_space=pltpu.HBM)] * (2 + len(tables)),
         out_specs=vmem,
         out_shape=jax.ShapeDtypeStruct((reach, groups, TILE, LANES), jnp.bfloat16),
-        scratch_shapes=[
+        scratch_shapes=[pltpu.VMEM(a.shape, a.dtype) for a in (frames_first, taps, *tables)]
+        + [
+            pltpu.SemaphoreType.DMA((7,)),
             pltpu.VMEM((per_chunk * inputs_here * outer, LANES), jnp.float32),
             pltpu.VMEM((width // LANES, kept * TILE, LANES), jnp.float32),
             pltpu.VMEM((chunks, kept, TILE, width), jnp.bfloat16),
@@ -401,7 +425,7 @@
         compiler_params=pltpu.CompilerParams(
             collective_id=0, has_side_effects=True, vmem_limit_bytes=48 * 2**20
         ),
-    )(jnp.transpose(voltages, (1, 0, 2)), taps, *tables)
+    )(frames_first, taps, *tables)
 
 
 def local(voltages, taps):
@@ -416,6 +440,7 @@
         and LANES % outer == 0
         and count % (2 * LANES // outer) == 0
         and count % TILE == 0
+        and count > 2 * LANES // outer
         and frame_len // 2 // outer % (n_stn * n_chan) == 0
         and (inputs_here * n_chan) ** 2 == SUB * LANES
     )

time: 83.2 us -> 84.4 us (1.014)
  Pallas kernels: 75.1 us -> 76.3 us
    pallas_call x1, Pallas kernels: 75.1 us -> 76.3 us  [fused(): pl.pallas_call(functools.partial(fused_kernel, n_stn, n_chan), in_specs=[...]
where the time goes in v2:
time: 84.4 us; the launch traced here: 84.1 us
  Pallas kernels  76.3 us (90%)
  local copies, waits for them, and re-layouts  7.74 us (9%)
    pallas_call x1, Pallas kernels, fused(): pl.pallas_call(functools.partial(fused_kernel, n_stn, n_chan), in_specs=[...  76.3 us
    unnamed x12, local copies, waits for them, and re-layouts  6.68 us

profile of v2, /device:TPU:0, one launch (start us, length us, event | category | flops | bytes accessed | tf_op | source)
XLA Modules:
  0.0 84.1 jit_solution(11680650400381010219)
XLA Ops:
  0.0 0.0 copy-start
  0.0 2.1 %copy-done = bf16[8,31,8192]{2,0,1:T(8,128)(2,1)S(1)} copy-done((bf16[8,31,8192]{2,0,1:T(8,128)(2,1)S(1)}, bf16[8,31,8192]{2,0,1:T(8,128)(2,1)}, u32[]{:S(2)}) %copy-start) | copy-done | bytes 4063256
  2.2 0.0 copy-start.1
  2.2 1.0 %copy-done.1 = f32[16,8192]{1,0:T(8,128)S(1)} copy-done((f32[16,8192]{1,0:T(8,128)S(1)}, f32[16,8192]{1,0:T(8,128)}, u32[]{:S(2)}) %copy-start.1) | copy-done | bytes 524312
  3.2 0.0 copy-start.2
  3.2 0.9 %copy-done.2 = bf16[4,16,1024]{2,1,0:T(8,128)(2,1)S(1)} copy-done((bf16[4,16,1024]{2,1,0:T(8,128)(2,1)S(1)}, bf16[4,16,1024]{2,1,0:T(8,128)(2,1)}, u32[]{:S(2)}) %copy-start.2) | copy-done | bytes 131096
  4.1 0.0 copy-start.3
  4.1 0.9 %copy-done.3 = bf16[2,128,256]{2,1,0:T(8,128)(2,1)S(1)} copy-done((bf16[2,128,256]{2,1,0:T(8,128)(2,1)S(1)}, bf16[2,128,256]{2,1,0:T(8,128)(2,1)}, u32[]{:S(2)}) %copy-start.3) | copy-done | bytes 131096
  5.0 0.0 copy-start.4
  5.0 0.8 copy-done.4
  5.8 0.0 copy-start.5
  5.8 0.8 copy-done.5
  6.7 76.3 %shard_map.64 = bf16[3,64,16,128]{3,2,1,0:T(8,128)(2,1)S(1)} custom-call(bf16[31,8,8192]{2,1,0:T(8,128)(2,1)S(1)} %bitcast.3, f32[16,8192]{1,0:T(8,128)S(1)} %copy-done.1, bf16[128,192]{1,0:T(8,128)(2,1)S(1)} %copy-done.5, f32[2,64,128]{2,1,0:T(8,128)S(1)} %copy-done.4, bf16[2,128,256]{2,1,0:T(8,128)(2,1)S(1)} %copy-done.3, bf16[4,16,1024]{2,1,0:T(8,128)(2,1)S(1)} %copy-done.2), custom_call_target="tpu_custom_call" | custom-call | tf_op jit(solution)/shard_map/pallas_call | solution.py:404
  83.0 1.1 %reshape.3 = bf16[1,3,64,2,1024]{4,3,2,1,0:T(2,128)(2,1)} reshape(bf16[3,64,16,128]{3,2,1,0:T(8,128)(2,1)S(1)} %shard_map.64) | data formatting | bytes 1572864 | tf_op jit(solution)/shard_map/reshape | solution.py:451
Async XLA Ops:
  0.0 2.2 %copy-start = (bf16[8,31,8192]{2,0,1:T(8,128)(2,1)S(1)}, bf16[8,31,8192]{2,0,1:T(8,128)(2,1)}, u32[]{:S(2)}) copy-start(bf16[8,31,8192]{2,0,1:T(8,128)(2,1)} %param.6) | copy-start | bytes 12189700
  2.2 1.0 %copy-start.1 = (f32[16,8192]{1,0:T(8,128)S(1)}, f32[16,8192]{1,0:T(8,128)}, u32[]{:S(2)}) copy-start(f32[16,8192]{1,0:T(8,128)} %taps_hbm.1) | copy-start | bytes 1572868
  3.2 0.9 %copy-start.2 = (bf16[4,16,1024]{2,1,0:T(8,128)(2,1)S(1)}, bf16[4,16,1024]{2,1,0:T(8,128)(2,1)}, u32[]{:S(2)}) copy-start(bf16[4,16,1024]{2,1,0:T(8,128)(2,1)} %constant.11.clone.mask_hbm) | copy-start | bytes 393220
  4.1 0.9 %copy-start.3 = (bf16[2,128,256]{2,1,0:T(8,128)(2,1)S(1)}, bf16[2,128,256]{2,1,0:T(8,128)(2,1)}, u32[]{:S(2)}) copy-start(bf16[2,128,256]{2,1,0:T(8,128)(2,1)} %constant.10.clone.last_hbm) | copy-start | bytes 393220
  5.0 0.8 copy-start.4
  5.8 0.8 copy-start.5

commit v3 on v2

--- a/solution.py
+++ b/solution.py
@@ -423,7 +423,7 @@
             pltpu.SemaphoreType.DMA((n_stn - 1, steps)),
         ],
         compiler_params=pltpu.CompilerParams(
-            collective_id=0, has_side_effects=True, vmem_limit_bytes=48 * 2**20
+            collective_id=0, has_side_effects=True, vmem_limit_bytes=63 * 2**20
         ),
     )(frames_first, taps, *tables)
 

time: 84.4 us -> 79.1 us (0.937)
  local copies, waits for them, and re-layouts: 7.74 us -> 2.71 us
    unnamed x12 -> x0, local copies, waits for them, and re-layouts: 6.68 us -> none
    reshape x1, local copies, waits for them, and re-layouts: 1.06 us -> 2.71 us  [local(): return tiles.reshape(1, reach, groups, 2, (inputs_here * n_chan) ** 2)]
where the time goes in v3:
time: 79.1 us; the launch traced here: 79 us
  Pallas kernels  76.2 us (96%)
  local copies, waits for them, and re-layouts  2.71 us (3%)
    pallas_call x1, Pallas kernels, fused(): pl.pallas_call(functools.partial(fused_kernel, n_stn, n_chan), in_specs=[...  76.2 us
    reshape x1, local copies, waits for them, and re-layouts, local(): return tiles.reshape(1, reach, groups, 2, (inputs_here * n_chan) ** 2)  2.71 us

profile of v3, /device:TPU:0, one launch (start us, length us, event | category | flops | bytes accessed | tf_op | source)
XLA Modules:
  0.0 79.0 jit_solution(13203499827351367716)
XLA Ops:
  0.0 76.2 %shard_map.64 = bf16[3,64,16,128]{3,2,1,0:T(8,128)(2,1)} custom-call(bf16[31,8,8192]{2,1,0:T(8,128)(2,1)} %bitcast.3, f32[16,8192]{1,0:T(8,128)} %taps_hbm.1, bf16[128,192]{1,0:T(8,128)(2,1)} %constant.8.clone.first_hbm, f32[2,64,128]{2,1,0:T(8,128)} %constant.9.clone.twist_hbm, bf16[2,128,256]{2,1,0:T(8,128)(2,1)} %constant.10.clone.last_hbm, ...), custom_call_target="tpu_custom_call" | custom-call | tf_op jit(solution)/shard_map/pallas_call | solution.py:404
  76.2 2.7 %reshape.3 = bf16[1,3,64,2,1024]{4,3,2,1,0:T(2,128)(2,1)} reshape(bf16[3,64,16,128]{3,2,1,0:T(8,128)(2,1)} %shard_map.64) | data formatting | bytes 1572864 | tf_op jit(solution)/shard_map/reshape | solution.py:451

commit v4 on v3

--- a/solution.py
+++ b/solution.py
@@ -158,6 +158,8 @@
     n_stn, n_chan, v_hbm, taps_hbm, first_hbm, twist_hbm, last_hbm, mask_hbm, out_ref,
     v_ref, taps_ref, first_ref, twist_ref, last_ref, mask_ref, in_sem, weighted, held, spec, got, pair, mine,
     own_sem, send_sem, recv_sem, back_own, back_send, back_recv,
+    near, near_pair, near_mine, near_own, near_send, near_recv,
+    near_back_own, near_back_send, near_back_recv,
 ):
     grp = lax.axis_index("grp")
     stn = lax.axis_index("stn")
@@ -175,6 +177,18 @@
     me = stn * n_chan + chan
     turns = [(a, b) for a in range(n_stn) for b in range(n_chan) if (a, b) != (0, 0)]
 
+    half = n_stn // 2
+    within = lax.rem(stn, half)
+    base = stn - within
+    me_near = within * n_chan + chan
+    near_turns = [(a, b) for a in range(half) for b in range(n_chan) if (a, b) != (0, 0)]
+
+    def twin(s):
+        return lax.rem(s + half, n_stn)
+
+    def neighbour(a):
+        return base + lax.rem(within + a, half)
+
     def partner(turn):
         return lax.rem(stn + turn[0], n_stn), lax.rem(chan + turn[1], n_chan)
 
@@ -219,28 +233,77 @@
             device_id_type=pl.DeviceIdType.MESH,
         )
 
+    def near_own_copy(chunk):
+        return pltpu.make_async_copy(
+            spec.at[chunk, pl.ds(first_row(twin(stn), chan), steps)],
+            near.at[chunk, me_near],
+            near_own.at[chunk],
+        )
+
+    def near_outgoing(n, chunk):
+        s, c = neighbour(near_turns[n][0]), lax.rem(chan + near_turns[n][1], n_chan)
+        return pltpu.make_async_remote_copy(
+            src_ref=spec.at[chunk, pl.ds(first_row(twin(s), c), steps)],
+            dst_ref=near.at[chunk, me_near],
+            send_sem=near_send.at[n, chunk],
+            recv_sem=near_recv.at[n, chunk],
+            device_id=(grp, s, c),
+            device_id_type=pl.DeviceIdType.MESH,
+        )
+
     groups_here = steps * sub_groups
 
-    def places(step):
+    def places(step, part):
         return pl.ds(step * sub_groups, sub_groups), pl.ds(
-            stn * groups_here + step * sub_groups, sub_groups
+            part * groups_here + step * sub_groups, sub_groups
         )
 
     def back_own_copy(step):
-        src, dst = places(step)
+        src, dst = places(step, stn)
         return pltpu.make_async_copy(mine.at[stn, :, src], out_ref.at[:, dst], back_own.at[step])
 
-    def going_back(n, step):
-        src, dst = places(step)
+    def going_back(n, d, step):
+        src, dst = places(step, stn)
         s = lax.rem(stn + n, n_stn)
         return pltpu.make_async_remote_copy(
-            src_ref=mine.at[s, :, src],
-            dst_ref=out_ref.at[:, dst],
-            send_sem=back_send.at[n - 1, step],
-            recv_sem=back_recv.at[n - 1, step],
+            src_ref=mine.at[s, d, src],
+            dst_ref=out_ref.at[d, dst],
+            send_sem=back_send.at[n - 1, d, step],
+            recv_sem=back_recv.at[n - 1, d, step],
             device_id=(grp, s, chan),
             device_id_type=pl.DeviceIdType.MESH,
         )
+
+    def near_back_own_copy(d, step):
+        src, dst = places(step, twin(stn))
+        return pltpu.make_async_copy(
+            near_mine.at[within, d, src], out_ref.at[d, dst], near_back_own.at[d, step]
+        )
+
+    def near_going_back(a, d, step):
+        src, dst = places(step, twin(stn))
+        s = neighbour(a)
+        return pltpu.make_async_remote_copy(
+            src_ref=near_mine.at[lax.rem(within + a, half), d, src],
+            dst_ref=out_ref.at[d, dst],
+            send_sem=near_back_send.at[a - 1, d, step],
+            recv_sem=near_back_recv.at[a - 1, d, step],
+            device_id=(grp, s, chan),
+            device_id_type=pl.DeviceIdType.MESH,
+        )
+
+    def owed(worker, owner, d):
+        place = lax.rem(owner, half)
+        same = worker - lax.rem(worker, half) == owner - place
+        return jnp.logical_or(same, place + d >= half)
+
+    def stays(owner, d):
+        return lax.rem(owner, half) + d < half
+
+    def each_back(act):
+        for n in range(1, n_stn):
+            for d in range(reach):
+                act(n, d)
 
     order = sorted(range(len(turns)), key=lambda n: turns[n][0] == 0)
 
@@ -316,6 +379,9 @@
         own_copy(chunk).start()
         for n in order:
             outgoing(n, chunk).start()
+        near_own_copy(chunk).start()
+        for n in range(len(near_turns)):
+            near_outgoing(n, chunk).start()
         return carry
 
     for copy in loads:
@@ -332,55 +398,135 @@
     n_rows = n_stn * n_chan * SUB
     lane_part = lax.broadcasted_iota(jnp.int32, (SUB, LANES), 1) // block
 
-    def one_step(step, carry):
+    def stack(buffer, step):
         columns = []
         for chunk in range(chunks):
-            both = got[chunk, :, step].astype(jnp.float32)
+            both = buffer[chunk, :, step].astype(jnp.float32)
+            rows = both.shape[0] * SUB
             columns.append(
                 jnp.concatenate(
-                    [both[:, :SUB, :].reshape(n_rows, width), both[:, SUB:, :].reshape(n_rows, width)],
+                    [both[:, :SUB, :].reshape(rows, width), both[:, SUB:, :].reshape(rows, width)],
                     axis=0,
                 ).astype(jnp.bfloat16)
             )
-        rows = jnp.concatenate(columns, axis=1)
+        return jnp.concatenate(columns, axis=1)
+
+    def products(rows, g):
         total = chunks * width
+        chosen = rows.reshape(rows.shape[0] // TILE, TILE, total) * mask_ref[g][None]
+        return rows_by_rows(chosen.reshape(rows.shape[0], total), rows)
+
+    def slabs_of(source, g, b):
+        return [
+            [source[g, part, pl.ds(b * block + e, SUB, stride=across), :] for e in range(across)]
+            for part in range(2)
+        ]
+
+    def flatten(slabs, other):
+        tiles = []
+        for part in range(2):
+            flat = None
+            for e in range(across):
+                shift = (e - other) % across * block
+                moved = pltpu.roll(slabs[part][e], shift, 1) if shift else slabs[part][e]
+                flat = moved if flat is None else jnp.where(lane_part == e, moved, flat)
+            tiles.append(flat)
+        return jnp.concatenate(tiles, axis=0).astype(jnp.bfloat16)
+
+    def one_step(step, carry):
+        rows = stack(got, step)
         for g in range(sub_groups):
-            chosen = rows.reshape(2 * n_rows // TILE, TILE, total) * mask_ref[g][None]
-            product = rows_by_rows(chosen.reshape(2 * n_rows, total), rows)
+            product = products(rows, g)
             pair[g, 0] = (product[:n_rows, :n_rows] + product[n_rows:, n_rows:]) * scale
             pair[g, 1] = (product[n_rows:, :n_rows] - product[:n_rows, n_rows:]) * scale
             for b in range(n_stn):
-                slabs = [
-                    [pair[g, part, pl.ds(b * block + e, SUB, stride=across), :] for e in range(across)]
-                    for part in range(2)
-                ]
+                slabs = slabs_of(pair, g, b)
                 for d in range(reach):
-                    other = (b + d) % n_stn
-                    tiles = []
-                    for part in range(2):
-                        flat = None
-                        for e in range(across):
-                            shift = (e - other) % across * block
-                            moved = pltpu.roll(slabs[part][e], shift, 1) if shift else slabs[part][e]
-                            flat = moved if flat is None else jnp.where(lane_part == e, moved, flat)
-                        tiles.append(flat)
-                    mine[b, d, step * sub_groups + g] = jnp.concatenate(tiles, axis=0).astype(
-                        jnp.bfloat16
-                    )
+                    mine[b, d, step * sub_groups + g] = flatten(slabs, (b + d) % n_stn)
         back_own_copy(step).start()
-        for n in range(1, n_stn):
-            going_back(n, step).start()
+
+        def send(n, d):
+            @pl.when(owed(stn, lax.rem(stn + n, n_stn), d))
+            def _():
+                going_back(n, d, step).start()
+
+        each_back(send)
         return carry
 
     lax.fori_loop(0, steps, one_step, 0)
+
+    for chunk in range(chunks):
+        near_own_copy(chunk).wait()
+        for n in range(len(near_turns)):
+            near_outgoing(n, chunk).wait_recv()
+
+    near_rows = half * n_chan * SUB
+
+    def near_step(step, carry):
+        rows = stack(near, step)
+        for g in range(sub_groups):
+            product = products(rows, g)
+            turned = pltpu.roll(product, near_rows, 1)
+            near_pair[g, 0] = (product[:near_rows] + turned[near_rows:]) * scale
+            near_pair[g, 1] = (product[near_rows:] - turned[:near_rows]) * scale
+            for b in range(half):
+                slabs = slabs_of(near_pair, g, b)
+                for d in range(half - b):
+                    near_mine[b, d, step * sub_groups + g] = flatten(slabs, b + d)
+        for d in range(half):
+
+            @pl.when(stays(stn, d))
+            def _():
+                near_back_own_copy(d, step).start()
+
+            for a in range(1, half):
+
+                @pl.when(stays(neighbour(a), d))
+                def _():
+                    near_going_back(a, d, step).start()
+
+        return carry
+
+    lax.fori_loop(0, steps, near_step, 0)
 
     for chunk in range(chunks):
         for n in range(len(turns)):
             outgoing(n, chunk).wait_send()
-    for step in range(steps):
+        for n in range(len(near_turns)):
+            near_outgoing(n, chunk).wait_send()
+
+    def finish(step, carry):
         back_own_copy(step).wait()
-        for n in range(1, n_stn):
-            going_back(n, step).wait()
+
+        def end(n, d):
+            @pl.when(owed(stn, lax.rem(stn + n, n_stn), d))
+            def _():
+                going_back(n, d, step).wait_send()
+
+            @pl.when(owed(lax.rem(stn - n + n_stn, n_stn), stn, d))
+            def _():
+                going_back(n, d, step).wait_recv()
+
+        each_back(end)
+        for d in range(half):
+
+            @pl.when(stays(stn, d))
+            def _():
+                near_back_own_copy(d, step).wait()
+
+            for a in range(1, half):
+
+                @pl.when(stays(neighbour(a), d))
+                def _():
+                    near_going_back(a, d, step).wait_send()
+
+                @pl.when(stays(stn, d))
+                def _():
+                    near_going_back(a, d, step).wait_recv()
+
+        return carry
+
+    lax.fori_loop(0, steps, finish, 0)
 
 
 def fused(voltages, taps, n_stn, n_chan):
@@ -394,7 +540,8 @@
     peers = n_stn * n_chan - 1
     steps = kept // (n_stn * n_chan)
     sub_groups = outer // AVG
-    reach = n_stn // 2 + 1
+    half = n_stn // 2
+    reach = half + 1
     groups = kept // n_chan * sub_groups
     mask = (np.arange(count * outer) % outer // AVG)[None, :] == np.arange(sub_groups)[:, None]
     mask = np.broadcast_to(mask[:, None, :], (sub_groups, TILE, count * outer)).astype(jnp.bfloat16)
@@ -419,8 +566,17 @@
             pltpu.SemaphoreType.DMA((peers, chunks)),
             pltpu.SemaphoreType.DMA((peers, chunks)),
             pltpu.SemaphoreType.DMA((steps,)),
-            pltpu.SemaphoreType.DMA((n_stn - 1, steps)),
-            pltpu.SemaphoreType.DMA((n_stn - 1, steps)),
+            pltpu.SemaphoreType.DMA((n_stn - 1, reach, steps)),
+            pltpu.SemaphoreType.DMA((n_stn - 1, reach, steps)),
+            pltpu.VMEM((chunks, half * n_chan, steps, TILE, width), jnp.bfloat16),
+            pltpu.VMEM((sub_groups, 2, half * n_chan * SUB, LANES), jnp.float32),
+            pltpu.VMEM((half, half, steps * sub_groups, TILE, LANES), jnp.bfloat16),
+            pltpu.SemaphoreType.DMA((chunks,)),
+            pltpu.SemaphoreType.DMA((half * n_chan - 1, chunks)),
+            pltpu.SemaphoreType.DMA((half * n_chan - 1, chunks)),
+            pltpu.SemaphoreType.DMA((half, steps)),
+            pltpu.SemaphoreType.DMA((half - 1, half, steps)),
+            pltpu.SemaphoreType.DMA((half - 1, half, steps)),
         ],
         compiler_params=pltpu.CompilerParams(
             collective_id=0, has_side_effects=True, vmem_limit_bytes=63 * 2**20
@@ -440,6 +596,8 @@
         and LANES % outer == 0
         and count % (2 * LANES // outer) == 0
         and count % TILE == 0
+        and n_stn % 2 == 0
+        and n_stn > 2
         and count > 2 * LANES // outer
         and frame_len // 2 // outer % (n_stn * n_chan) == 0
         and (inputs_here * n_chan) ** 2 == SUB * LANES

time: 79.1 us -> 75.5 us (0.954)
  Pallas kernels: 76.2 us -> 72.6 us
    pallas_call x1, Pallas kernels: 76.2 us -> 72.6 us  [fused(): pl.pallas_call(functools.partial(fused_kernel, n_stn, n_chan), in_specs=[...]
where the time goes in v4:
time: 75.5 us; the launch traced here: 75.3 us
  Pallas kernels  72.6 us (96%)
  local copies, waits for them, and re-layouts  2.71 us (4%)
    pallas_call x1, Pallas kernels, fused(): pl.pallas_call(functools.partial(fused_kernel, n_stn, n_chan), in_specs=[...  72.6 us
    reshape x1, local copies, waits for them, and re-layouts, local(): return tiles.reshape(1, reach, groups, 2, (inputs_here * n_chan) ** 2)  2.71 us

profile of v4, /device:TPU:0, one launch (start us, length us, event | category | flops | bytes accessed | tf_op | source)
XLA Modules:
  0.0 75.3 jit_solution(6043000480599789174)
XLA Ops:
  0.0 72.6 %shard_map.64 = bf16[3,64,16,128]{3,2,1,0:T(8,128)(2,1)} custom-call(bf16[31,8,8192]{2,1,0:T(8,128)(2,1)} %bitcast.3, f32[16,8192]{1,0:T(8,128)} %taps_hbm.1, bf16[128,192]{1,0:T(8,128)(2,1)} %constant.8.clone.first_hbm, f32[2,64,128]{2,1,0:T(8,128)} %constant.9.clone.twist_hbm, bf16[2,128,256]{2,1,0:T(8,128)(2,1)} %constant.10.clone.last_hbm, ...), custom_call_target="tpu_custom_call" | custom-call | tf_op jit(solution)/shard_map/pallas_call | solution.py:551
  72.6 2.7 %reshape.3 = bf16[1,3,64,2,1024]{4,3,2,1,0:T(2,128)(2,1)} reshape(bf16[3,64,16,128]{3,2,1,0:T(8,128)(2,1)} %shard_map.64) | data formatting | bytes 1572864 | tf_op jit(solution)/shard_map/reshape | solution.py:609

commit v5 on v4

--- a/solution.py
+++ b/solution.py
@@ -376,23 +376,18 @@
             spec[chunk, :, :, k * LANES : (k + 1) * LANES] = (
                 held[k].reshape(kept, TILE, LANES).astype(jnp.bfloat16)
             )
+        near_own_copy(chunk).start()
+        for n in range(len(near_turns)):
+            near_outgoing(n, chunk).start()
         own_copy(chunk).start()
         for n in order:
             outgoing(n, chunk).start()
-        near_own_copy(chunk).start()
-        for n in range(len(near_turns)):
-            near_outgoing(n, chunk).start()
         return carry
 
     for copy in loads:
         copy.wait()
     lax.fori_loop(0, chunks, one_chunk, 0)
     last_load.wait()
-
-    for chunk in range(chunks):
-        own_copy(chunk).wait()
-        for n in range(len(turns)):
-            outgoing(n, chunk).wait_recv()
 
     scale = 1.0 / (count * AVG)
     n_rows = n_stn * n_chan * SUB
@@ -453,8 +448,6 @@
         each_back(send)
         return carry
 
-    lax.fori_loop(0, steps, one_step, 0)
-
     for chunk in range(chunks):
         near_own_copy(chunk).wait()
         for n in range(len(near_turns)):
@@ -488,6 +481,13 @@
         return carry
 
     lax.fori_loop(0, steps, near_step, 0)
+
+    for chunk in range(chunks):
+        own_copy(chunk).wait()
+        for n in range(len(turns)):
+            outgoing(n, chunk).wait_recv()
+
+    lax.fori_loop(0, steps, one_step, 0)
 
     for chunk in range(chunks):
         for n in range(len(turns)):

time: 75.5 us -> 75.7 us (level)
  no operation moved by 1% of the time
where the time goes in v5:
time: 75.7 us; the launch traced here: 75.5 us
  Pallas kernels  72.8 us (96%)
  local copies, waits for them, and re-layouts  2.71 us (4%)
    pallas_call x1, Pallas kernels, fused(): pl.pallas_call(functools.partial(fused_kernel, n_stn, n_chan), in_specs=[...  72.8 us
    reshape x1, local copies, waits for them, and re-layouts, local(): return tiles.reshape(1, reach, groups, 2, (inputs_here * n_chan) ** 2)  2.71 us

profile of v5, /device:TPU:0, one launch (start us, length us, event | category | flops | bytes accessed | tf_op | source)
XLA Modules:
  0.0 75.5 jit_solution(14922124803467978739)
XLA Ops:
  0.0 72.8 %shard_map.64 = bf16[3,64,16,128]{3,2,1,0:T(8,128)(2,1)} custom-call(bf16[31,8,8192]{2,1,0:T(8,128)(2,1)} %bitcast.3, f32[16,8192]{1,0:T(8,128)} %taps_hbm.1, bf16[128,192]{1,0:T(8,128)(2,1)} %constant.8.clone.first_hbm, f32[2,64,128]{2,1,0:T(8,128)} %constant.9.clone.twist_hbm, bf16[2,128,256]{2,1,0:T(8,128)(2,1)} %constant.10.clone.last_hbm, ...), custom_call_target="tpu_custom_call" | custom-call | tf_op jit(solution)/shard_map/pallas_call | solution.py:551
  72.8 2.7 %reshape.3 = bf16[1,3,64,2,1024]{4,3,2,1,0:T(2,128)(2,1)} reshape(bf16[3,64,16,128]{3,2,1,0:T(8,128)(2,1)} %shard_map.64) | data formatting | bytes 1572864 | tf_op jit(solution)/shard_map/reshape | solution.py:609
